TPU v7x, 768 devices: a whole 4x8x12 slice. The times are simulated.
768 devices in a mesh: dp: 96 (over z, x, core), group: 8 (over y).
Axes of the slice: x: 4, y: 8, z: 12, core: 2. Of those that a mesh axis runs over, the one named last changes fastest.
Arguments:
- partials: bfloat16 [96, 2304, 2048], P('dp', None, 'group')
- momentum: float32 [2304, 2048], P('dp', 'group'), may hold values from -6 to 6
Outputs:
- update: float32 [2304, 2048], P('dp', 'group')
- new_momentum: float32 [2304, 2048], P('dp', 'group')
All inputs are finite; a program needn't handle non-finite values.
Results may differ from a plain program's by a relative error of at most 0.0003.
Values sent between devices are 32-bit elements; how exact they have to be, the bound alone decides.
No kernel may reach another device: no remote copies, remote signals or barrier semaphores. Data moves between devices by JAX's collectives and lax.ppermute only.
A program may use at most 32 MiB of HBM per device.

v0:
```python
import functools
import math

import jax
import jax.numpy as jnp
import numpy as np
from jax import lax
from jax.experimental import pallas as pl
from jax.experimental.pallas import tpu as pltpu
from jax.sharding import Mesh
from jax.sharding import PartitionSpec as P

D = 2048
KV_ROWS = 576
MATS = 4
PADDED = 640
TILE = 128

coef_a = 3.4445
coef_b = -4.775
coef_c = 2.0315

GAIN = 1.95
KAPPA = 0.9025 / 1.95

BLOCK = 64

STRIPS = [((0, 0), (8, 8))]
STRIPS += [
    ((i, 2 * j), (i, 2 * j + 1))
    for i in range(1, 9)
    for j in range(i // 2 + 1)
    if (i, j) != (8, 4)
]
STARTS = [next(n for n, (a, _) in enumerate(STRIPS) if a[0] == i) for i in range(9)]
PAIRS = [(i, j) for i in range(5) for j in range(i + 1)]

CHUNKS = 4
SPLIT_LIMIT = 53739520

VMEM = pl.BlockSpec(memory_space=pltpu.VMEM)
HBM = pl.BlockSpec(memory_space=pltpu.HBM)
SMEM = pl.BlockSpec(memory_space=pltpu.SMEM)
NT = (((1,), (1,)), ((), ()))
NN = (((1,), (0,)), ((), ()))


def split_kernel(
    place_ref, partial_ref, momentum_ref, keep_ref, send_ref, raw, held, low, high, sems
):
    core, position = place_ref[0], place_ref[1]
    chunk = raw.shape[0] // CHUNKS
    copies = [pltpu.make_async_copy(momentum_ref, held, sems.at[CHUNKS])]
    for q in range(CHUNKS):
        rows = pl.ds(q * chunk, chunk)
        copies.append(pltpu.make_async_copy(partial_ref.at[rows], raw.at[rows], sems.at[q]))
    for copy in copies:
        copy.start()
    copies[0].wait()
    own = position * 24
    for q in range(CHUNKS):
        copies[q + 1].wait()
        rows = slice(q * chunk, (q + 1) * chunk)
        low[rows, :] = raw[rows, :TILE].astype(jnp.float32)
        high[rows, :] = raw[rows, TILE:].astype(jnp.float32)

        @pl.when(own // chunk == q)
        def _():
            mine = pl.ds(pl.multiple_of(own, 8), 24)
            low[mine, :] += KAPPA * held[:, :TILE]
            high[mine, :] += KAPPA * held[:, TILE:]

        def put(mine, other):
            for m in range(MATS):
                rows = pl.ds(q * chunk + m, chunk // MATS, stride=MATS)
                groups = slice(q * 12 // CHUNKS, (q + 1) * 12 // CHUNKS)
                keep_ref[groups, m] = mine[rows, :].reshape(-1, 48, TILE)
                send_ref[groups, m] = other[rows, :].reshape(-1, 48, TILE)

        @pl.when(core == 0)
        def _():
            put(low, high)

        @pl.when(core == 1)
        def _():
            put(high, low)


def split(place, partial, momentum):
    half = jax.ShapeDtypeStruct((12, MATS, 48, TILE), jnp.float32)
    return pl.pallas_call(
        split_kernel,
        out_shape=(half, half),
        in_specs=[SMEM, HBM, HBM],
        out_specs=(VMEM, VMEM),
        scratch_shapes=[
            pltpu.VMEM((MATS * KV_ROWS, 2 * TILE), jnp.bfloat16),
            pltpu.VMEM((24, 2 * TILE), jnp.float32),
        ]
        + [pltpu.VMEM((MATS * KV_ROWS, TILE), jnp.float32)] * 2
        + [pltpu.SemaphoreType.DMA((CHUNKS + 1,))],
        compiler_params=pltpu.CompilerParams(vmem_limit_bytes=SPLIT_LIMIT),
    )(place, partial, momentum)


def gram_kernel(place_ref, halves_ref, out_ref):
    strip = place_ref[3]
    i, start = jnp.int32(0), jnp.int32(0)
    for begin, step in zip(STARTS[1:], np.diff(STARTS)):
        past = strip >= begin
        i += past.astype(jnp.int32)
        start += jnp.where(past, int(step), 0)
    j = 2 * (strip - start)
    ends = strip == 0
    sides = [(i, j), (jnp.where(ends, 8, i), jnp.where(ends, 8, j + 1))]
    for side, pair in enumerate(sides):
        picks = [pl.ds(pl.multiple_of(k * BLOCK, BLOCK), BLOCK) for k in pair]
        left, right = (
            jnp.concatenate([halves_ref[0, rows, :], halves_ref[1, rows, :]], 1) for rows in picks
        )
        left_top, left_middle, _ = three(left)
        right_top, right_middle, _ = three(right)
        dot = functools.partial(
            lax.dot_general, dimension_numbers=NT, preferred_element_type=jnp.float32
        )
        both = dot(jnp.concatenate([left_top, left_middle], 0), right_top)
        small = both[BLOCK:] + dot(left_top, right_middle)
        out_ref[:, side * BLOCK : (side + 1) * BLOCK] = both[:BLOCK] + small


def gram(place, halves):
    return pl.pallas_call(
        gram_kernel,
        out_shape=jax.ShapeDtypeStruct((BLOCK, TILE), jnp.float32),
        in_specs=[SMEM, VMEM],
        out_specs=VMEM,
        compiler_params=pltpu.CompilerParams(vmem_limit_bytes=24 << 20),
    )(place, halves)


def three(x):
    top = x.astype(jnp.bfloat16)
    rest = x - top.astype(jnp.float32)
    middle = rest.astype(jnp.bfloat16)
    bottom = (rest - middle.astype(jnp.float32)).astype(jnp.bfloat16)
    return top, middle, bottom


def times(x, right):
    n, count = x.shape[0], len(right)
    parts = three(x)
    total = 0.0
    for at, ref in reversed(list(enumerate(right))):
        product = lax.dot_general(
            jnp.concatenate(parts[: count - at], 0),
            ref[...],
            NN,
            preferred_element_type=jnp.float32,
        )
        for k in reversed(range(count - at)):
            total = total + product[k * n : (k + 1) * n]
    return total


def triangle(strips_ref):
    zero = jnp.zeros((BLOCK, BLOCK), jnp.float32)
    strip = {}
    for at, ((i, j), other) in enumerate(STRIPS[1:], 1):
        strip[i, j // 2] = strips_ref[at]
    ends = strips_ref[0]
    strip[0, 0] = jnp.concatenate([ends[:, :BLOCK], strip[1, 0][:, :BLOCK].T], 1)
    strip[8, 4] = jnp.concatenate([ends[:, BLOCK:], zero], 1)
    blank = jnp.concatenate([zero, zero], 1)
    return {
        (i, j): jnp.concatenate([strip[2 * i, j], strip.get((2 * i + 1, j), blank)], 0)
        for i, j in PAIRS
    }


def chain_kernel(place_ref, strips_ref, halves_ref, out_ref, g0, g1, t0, t1, t2):
    first_row = place_ref[2]
    blocks = triangle(strips_ref)
    row = lax.broadcasted_iota(jnp.int32, (TILE, TILE), 0)
    column = lax.broadcasted_iota(jnp.int32, (TILE, TILE), 1)
    diagonal = jnp.zeros((TILE, TILE), jnp.float32)
    for i in range(5):
        diagonal += jnp.where(row == column, blocks[i, i], 0.0)
    squares = jnp.sum(jnp.sum(diagonal, axis=0, keepdims=True), axis=1, keepdims=True)
    scale = GAIN / (GAIN * jnp.sqrt(squares) + 1e-07)
    for i, j in PAIRS:
        block = (blocks[i, j] * scale) * scale
        here = (slice(i * TILE, (i + 1) * TILE), slice(j * TILE, (j + 1) * TILE))
        for ref, part in zip((g0, g1), three(block)):
            ref[here] = part
        if i != j:
            for ref, part in zip((g0, g1), three(block.T)):
                ref[here[1], here[0]] = part
    for half in range(2):
        for ref, part in zip((t0, t1, t2), three(halves_ref[half])):
            ref[:KV_ROWS, half * TILE : (half + 1) * TILE] = part
    for ref in (t0, t1, t2):
        ref[KV_ROWS:, :] = jnp.zeros((PADDED - KV_ROWS, 2 * TILE), jnp.bfloat16)
    g, t = (g0, g1), (t0, t1, t2)

    r = lax.broadcasted_iota(jnp.int32, (32, PADDED), 0)
    k = lax.broadcasted_iota(jnp.int32, (32, PADDED), 1)
    wanted = first_row + 144 * (r >> 3) + (r & 7)
    pick = jnp.where(jnp.logical_and(k == wanted, (r & 7) < 6), 1.0, 0.0)

    def poly(x):
        once = times(x, g)
        return coef_a * x + coef_b * once + coef_c * times(once, g)

    first = poly(pick)
    second = times(poly(poly(first)), g)
    third = times(poly(poly(second)), g)
    rows = coef_a * first + coef_b * second + coef_c * third
    gain = (0.2 * math.sqrt(max(KV_ROWS, D))) * scale
    both = times(jnp.concatenate([rows, pick], 0), t)
    update, own = gain * both[:32], both[32:]
    for x in range(4):
        out_ref[x, :8, :] = update[8 * x : 8 * x + 8]
        out_ref[x, 8:, :] = own[8 * x : 8 * x + 8]


def chain(place, strips, halves):
    return pl.pallas_call(
        chain_kernel,
        out_shape=jax.ShapeDtypeStruct((4, 16, 2 * TILE), jnp.float32),
        in_specs=[SMEM, VMEM, VMEM],
        out_specs=VMEM,
        scratch_shapes=[pltpu.VMEM((PADDED, PADDED), jnp.bfloat16)] * 2
        + [pltpu.VMEM((PADDED, 2 * TILE), jnp.bfloat16)] * 3,
        compiler_params=pltpu.CompilerParams(vmem_limit_bytes=24 << 20),
    )(place, strips, halves)


def finish_kernel(got_ref, momentum_ref, update_ref, new_ref, update_half, sum_half):
    for half in range(2):
        columns = slice(half * TILE, (half + 1) * TILE)
        for m in range(MATS):
            rows = pl.ds(m, 6, stride=MATS)
            update_half[rows, :] = got_ref[m, 0:6, columns]
            sum_half[rows, :] = got_ref[m, 8:14, columns]
        momentum = momentum_ref[:, columns]
        update_ref[:, columns] = update_half[...]
        new_ref[:, columns] = 0.95 * momentum + (sum_half[...] - KAPPA * momentum)


def finish(got, momentum):
    shape = jax.ShapeDtypeStruct(momentum.shape, jnp.float32)
    return pl.pallas_call(
        finish_kernel,
        out_shape=(shape, shape),
        in_specs=[VMEM, VMEM],
        out_specs=(VMEM, VMEM),
        scratch_shapes=[pltpu.VMEM((24, TILE), jnp.float32)] * 2,
        compiler_params=pltpu.CompilerParams(vmem_limit_bytes=4 << 20),
    )(got, momentum)


def exchange(x, axis):
    return lax.all_to_all(x, axis, split_axis=0, concat_axis=0, tiled=True)


def spread(x, axis, count):
    return exchange(jnp.broadcast_to(x[None], (count, *x.shape)), axis)


def per_device(partials, momentum):
    w, v, x, c = (lax.axis_index(name) for name in ("w", "v", "x", "c"))
    z = 3 * w + v
    first_row = 48 * v + 12 * x + 6 * c
    strip = c * 12 + v * 4 + x
    place = jnp.stack([c, (z * 4 + x) * 2 + c, first_row, strip]).astype(jnp.int32)
    keep, send = split(place, partials[0], momentum)
    got = lax.ppermute(send, "c", [(0, 1), (1, 0)])
    near = jnp.sum(exchange(keep + got, ("v", "x")), axis=0)
    own = jnp.sum(exchange(near, "w"), axis=0)
    half = spread(own, ("v", "x"), 12).reshape(KV_ROWS, TILE)
    halves = lax.all_gather(half, "c", axis=0, tiled=False)
    mine = jnp.sum(spread(gram(place, halves), "y", 8), axis=0)
    strips = lax.all_gather(spread(mine, ("v", "x"), 12), "c", axis=0, tiled=True)
    done = chain(place, strips, halves)
    return finish(exchange(done, "w"), momentum)


def solution(mesh):
    fine = Mesh(mesh.devices.reshape(4, 3, 4, 2, 8), ("w", "v", "x", "c", "y"))
    rows = ("w", "v", "x", "c")
    return jax.shard_map(
        per_device,
        mesh=fine,
        in_specs=(P(rows, None, "y"), P(rows, "y")),
        out_specs=(P(rows, "y"), P(rows, "y")),
        check_vma=False,
    )
```

profile of v0, /device:TPU:1, one launch (start us, length us, event | category | flops | bytes accessed | tf_op | source)
XLA Modules:
  0.0 132.5 jit_solution(7709827333883323864)
XLA Ops:
  0.7 0.1 pad_add_fusion.place_ref
  0.7 0.0 copy-start
  0.7 0.7 copy-done
  1.5 1.9 %shard_map.41 = (f32[12,4,48,128]{3,2,1,0:T(8,128)S(1)}, f32[12,4,48,128]{3,2,1,0:T(8,128)S(1)}) custom-call(s32[4]{0:T(128)S(1)} %pad_add_fusion.place_ref, bf16[2304,256]{1,0:T(8,128)(2,1)} %bitcast.7, f32[24,256]{1,0:T(8,128)S(1)} %copy-done), custom_call_target="tpu_custom_call" | custom-call | tf_op jit(solution)/shard_map/pallas_call | solution.py:91
  3.4 12.4 %collective-permute-start = (f32[12,4,48,128]{3,2,1,0:T(8,128)S(1)}, f32[12,4,48,128]{3,2,1,0:T(8,128)S(1)}, u32[]{:S(2)}, u32[]{:S(2)}) collective-permute-start(f32[12,4,48,128]{3,2,1,0:T(8,128)S(1)} %get-tuple-element.5), channel_id=1, source_target_pairs={{0,8},{8,0},{1,9},{9,1},{2,10},{10,2},{3,11},{11,3},{4,12},{12,4},... | collective-permute-start | bytes 3538952 | tf_op jit(solution)/shard_map/ppermute | solution.py:277
  15.8 2.5 %collective-permute-done = f32[12,4,48,128]{3,2,1,0:T(8,128)S(1)} collective-permute-done((f32[12,4,48,128]{3,2,1,0:T(8,128)S(1)}, f32[12,4,48,128]{3,2,1,0:T(8,128)S(1)}, u32[]{:S(2)}, u32[]{:S(2)}) %collective-permute-start) | collective-permute-done | bytes 1179680 | tf_op jit(solution)/shard_map/ppermute | solution.py:277
  18.3 0.1 add.31
  18.4 22.1 %all_to_all.30 = f32[12,4,48,128]{3,2,1,0:T(8,128)S(1)} all-to-all(f32[12,4,48,128]{3,2,1,0:T(8,128)S(1)} %add.31), channel_id=1, replica_groups=mesh['w'=4,'v'=3,'x'=4,'c'=2,'y'=8] {'v','x'}, dimensions={0} | all-to-all | bytes 2359296 | tf_op jit(solution)/shard_map/all_to_all | solution.py:263
  40.5 0.1 reduce_sum.27
  40.6 18.8 %all_to_all.31 = f32[4,48,128]{2,1,0:T(8,128)S(1)} all-to-all(f32[4,48,128]{2,1,0:T(8,128)S(1)} %reduce_sum.27), channel_id=1, replica_groups=mesh['w'=4,'v'=3,'x'=4,'c'=2,'y'=8] {'w'}, dimensions={0} | all-to-all | bytes 196608 | tf_op jit(solution)/shard_map/all_to_all | solution.py:263
  59.4 11.9 %all_to_all.32 = f32[12,48,128]{2,1,0:T(8,128)S(1)} all-to-all(f32[12,48,128]{2,1,0:T(8,128)S(1)} %broadcast_in_dim.6), channel_id=1, replica_groups=mesh['w'=4,'v'=3,'x'=4,'c'=2,'y'=8] {'v','x'}, dimensions={0} | all-to-all | bytes 589824 | tf_op jit(solution)/shard_map/all_to_all | solution.py:263
  71.3 6.3 %all_gather.6.halves_ref = f32[2,576,128]{2,1,0:T(8,128)S(1)} all-gather(f32[1,576,128]{2,1,0:T(8,128)S(1)} %bitcast.6), channel_id=1, replica_groups=mesh['w'=4,'v'=3,'x'=4,'c'=2,'y'=8] {'c'}, dimensions={0}, use_global_device_ids=true | all-gather | bytes 884736 | tf_op jit(solution)/shard_map/all_gather | solution.py:281
  77.6 0.8 shard_map.42
  78.4 17.7 %all_to_all.33 = f32[8,64,128]{2,1,0:T(8,128)S(1)} all-to-all(f32[8,64,128]{2,1,0:T(8,128)S(1)} %broadcast_in_dim.7), channel_id=1, replica_groups=mesh['w'=4,'v'=3,'x'=4,'c'=2,'y'=8] {'y'}, dimensions={0} | all-to-all | bytes 524288 | tf_op jit(solution)/shard_map/all_to_all | solution.py:263
  96.2 10.5 %all_to_all.34 = f32[12,64,128]{2,1,0:T(8,128)S(1)} all-to-all(f32[12,64,128]{2,1,0:T(8,128)S(1)} %broadcast_in_dim.8), channel_id=1, replica_groups=mesh['w'=4,'v'=3,'x'=4,'c'=2,'y'=8] {'v','x'}, dimensions={0} | all-to-all | bytes 786432 | tf_op jit(solution)/shard_map/all_to_all | solution.py:263
  106.7 0.0 copy-start.1
  106.7 5.5 %all_gather.7.strips_ref = f32[24,64,128]{2,1,0:T(8,128)S(1)} all-gather(f32[12,64,128]{2,1,0:T(8,128)S(1)} %all_to_all.34), channel_id=1, replica_groups=mesh['w'=4,'v'=3,'x'=4,'c'=2,'y'=8] {'c'}, dimensions={0}, use_global_device_ids=true | all-gather | bytes 1179648 | tf_op jit(solution)/shard_map/all_gather | solution.py:283
  112.2 5.3 %shard_map.43 = f32[4,16,256]{2,1,0:T(8,128)S(1)} custom-call(s32[4]{0:T(128)S(1)} %pad_add_fusion.place_ref, f32[24,64,128]{2,1,0:T(8,128)S(1)} %all_gather.7.strips_ref, f32[2,576,128]{2,1,0:T(8,128)S(1)} %all_gather.6.halves_ref), custom_call_target="tpu_custom_call" | custom-call | tf_op jit(solution)/shard_map/pallas_call | solution.py:227
  117.5 14.4 %all_to_all.35.got_ref = f32[4,16,256]{2,1,0:T(8,128)S(1)} all-to-all(f32[4,16,256]{2,1,0:T(8,128)S(1)} %shard_map.43), channel_id=1, replica_groups=mesh['w'=4,'v'=3,'x'=4,'c'=2,'y'=8] {'w'}, dimensions={0} | all-to-all | bytes 131072 | tf_op jit(solution)/shard_map/all_to_all | solution.py:263
  131.9 0.0 copy-done.1
  131.9 0.6 shard_map.44
  (5 shorter events, 0.1 us)
Async XLA Ops:
  0.7 0.7 copy-start
  3.4 14.9 %collective-permute-start = (f32[12,4,48,128]{3,2,1,0:T(8,128)S(1)}, f32[12,4,48,128]{3,2,1,0:T(8,128)S(1)}, u32[]{:S(2)}, u32[]{:S(2)}) collective-permute-start(f32[12,4,48,128]{3,2,1,0:T(8,128)S(1)} %get-tuple-element.5), channel_id=1, source_target_pairs={{0,8},{8,0},{1,9},{9,1},{2,10},{10,2},{3,11},{11,3},{4,12},{12,4},... | collective-permute-start | bytes 3538952 | tf_op jit(solution)/shard_map/ppermute | solution.py:277
  106.7 25.2 %copy-start.1 = (f32[24,256]{1,0:T(8,128)S(1)}, f32[24,256]{1,0:T(8,128)}, u32[]{:S(2)}) copy-start(f32[24,256]{1,0:T(8,128)} %momentum_ref.3) | copy-start | bytes 73732
where the time goes:
time: 133 us
  blocking collectives  107 us (80%)
  starting transfers between devices  12.4 us (9%)
  Pallas kernels  8.69 us (7%)
  waiting for transfers between devices  2.45 us (2%)
    all_to_all x6, blocking collectives, exchange(): return lax.all_to_all(x, axis, split_axis=0, concat_axis=0, tiled=True)  95.4 us
    ppermute x1, starting transfers between devices, per_device(): got = lax.ppermute(send, 'c', [(0, 1), (1, 0)])  12.4 us
    all_gather x1, blocking collectives, per_device(): halves = lax.all_gather(half, 'c', axis=0, tiled=False)  6.28 us
    all_gather x1, blocking collectives, per_device(): lax.all_gather(spread(mine, ('v', 'x'), 12), 'c', axis=0, tiled=True)  5.47 us
    pallas_call x1, Pallas kernels, chain(): pl.pallas_call(chain_kernel, out_shape=jax.ShapeDtypeStruct((4, 16, 2 * T...  5.32 us
  transfers between devices with their start and end apart: 1, of which 1 were waited for; matrix products, arithmetic and copies ran while one was open for 0% of the time, Pallas kernels for 0%

commit v1 on v0

--- a/solution.py
+++ b/solution.py
@@ -271,16 +271,16 @@
     w, v, x, c = (lax.axis_index(name) for name in ("w", "v", "x", "c"))
     z = 3 * w + v
     first_row = 48 * v + 12 * x + 6 * c
-    strip = c * 12 + v * 4 + x
+    strip = c * 12 + x * 3 + v
     place = jnp.stack([c, (z * 4 + x) * 2 + c, first_row, strip]).astype(jnp.int32)
     keep, send = split(place, partials[0], momentum)
     got = lax.ppermute(send, "c", [(0, 1), (1, 0)])
-    near = jnp.sum(exchange(keep + got, ("v", "x")), axis=0)
+    near = jnp.sum(exchange(keep + got, ("x", "v")), axis=0)
     own = jnp.sum(exchange(near, "w"), axis=0)
-    half = spread(own, ("v", "x"), 12).reshape(KV_ROWS, TILE)
+    half = spread(own, ("x", "v"), 12).reshape(KV_ROWS, TILE)
     halves = lax.all_gather(half, "c", axis=0, tiled=False)
     mine = jnp.sum(spread(gram(place, halves), "y", 8), axis=0)
-    strips = lax.all_gather(spread(mine, ("v", "x"), 12), "c", axis=0, tiled=True)
+    strips = lax.all_gather(spread(mine, ("x", "v"), 12), "c", axis=0, tiled=True)
     done = chain(place, strips, halves)
     return finish(exchange(done, "w"), momentum)
 

time: 133 us -> 133 us (level)
  no operation moved by 1% of the time
where the time goes in v1:
time: 133 us
  blocking collectives  108 us (81%)
  starting transfers between devices  12.4 us (9%)
  Pallas kernels  8.69 us (7%)
  waiting for transfers between devices  2.45 us (2%)
    all_to_all x6, blocking collectives, exchange(): return lax.all_to_all(x, axis, split_axis=0, concat_axis=0, tiled=True)  95.8 us
    ppermute x1, starting transfers between devices, per_device(): got = lax.ppermute(send, 'c', [(0, 1), (1, 0)])  12.4 us
    all_gather x1, blocking collectives, per_device(): halves = lax.all_gather(half, 'c', axis=0, tiled=False)  6.4 us
    all_gather x1, blocking collectives, per_device(): lax.all_gather(spread(mine, ('x', 'v'), 12), 'c', axis=0, tiled=True)  5.37 us
    pallas_call x1, Pallas kernels, chain(): pl.pallas_call(chain_kernel, out_shape=jax.ShapeDtypeStruct((4, 16, 2 * T...  5.32 us
  transfers between devices with their start and end apart: 1, of which 1 were waited for; matrix products, arithmetic and copies ran while one was open for 0% of the time, Pallas kernels for 0%

profile of v1, /device:TPU:1, one launch (start us, length us, event | category | flops | bytes accessed | tf_op | source)
XLA Modules:
  0.0 132.9 jit_solution(5169625845655019908)
XLA Ops:
  0.7 0.1 pad_add_fusion.place_ref
  0.7 0.0 copy-start
  0.7 0.7 copy-done
  1.5 1.9 %shard_map.41 = (f32[12,4,48,128]{3,2,1,0:T(8,128)S(1)}, f32[12,4,48,128]{3,2,1,0:T(8,128)S(1)}) custom-call(s32[4]{0:T(128)S(1)} %pad_add_fusion.place_ref, bf16[2304,256]{1,0:T(8,128)(2,1)} %bitcast.7, f32[24,256]{1,0:T(8,128)S(1)} %copy-done), custom_call_target="tpu_custom_call" | custom-call | tf_op jit(solution)/shard_map/pallas_call | solution.py:91
  3.4 12.4 %collective-permute-start = (f32[12,4,48,128]{3,2,1,0:T(8,128)S(1)}, f32[12,4,48,128]{3,2,1,0:T(8,128)S(1)}, u32[]{:S(2)}, u32[]{:S(2)}) collective-permute-start(f32[12,4,48,128]{3,2,1,0:T(8,128)S(1)} %get-tuple-element.5), channel_id=1, source_target_pairs={{0,8},{8,0},{1,9},{9,1},{2,10},{10,2},{3,11},{11,3},{4,12},{12,4},... | collective-permute-start | bytes 3538952 | tf_op jit(solution)/shard_map/ppermute | solution.py:277
  15.8 2.5 %collective-permute-done = f32[12,4,48,128]{3,2,1,0:T(8,128)S(1)} collective-permute-done((f32[12,4,48,128]{3,2,1,0:T(8,128)S(1)}, f32[12,4,48,128]{3,2,1,0:T(8,128)S(1)}, u32[]{:S(2)}, u32[]{:S(2)}) %collective-permute-start) | collective-permute-done | bytes 1179680 | tf_op jit(solution)/shard_map/ppermute | solution.py:277
  18.3 0.1 add.31
  18.4 24.0 %all_to_all.30 = f32[12,4,48,128]{3,2,1,0:T(8,128)S(1)} all-to-all(f32[12,4,48,128]{3,2,1,0:T(8,128)S(1)} %add.31), channel_id=1, replica_groups=mesh['w'=4,'v'=3,'x'=4,'c'=2,'y'=8] {'x','v'}, dimensions={0} | all-to-all | bytes 2359296 | tf_op jit(solution)/shard_map/all_to_all | solution.py:263
  42.4 0.1 reduce_sum.27
  42.5 19.1 %all_to_all.31 = f32[4,48,128]{2,1,0:T(8,128)S(1)} all-to-all(f32[4,48,128]{2,1,0:T(8,128)S(1)} %reduce_sum.27), channel_id=1, replica_groups=mesh['w'=4,'v'=3,'x'=4,'c'=2,'y'=8] {'w'}, dimensions={0} | all-to-all | bytes 196608 | tf_op jit(solution)/shard_map/all_to_all | solution.py:263
  61.6 10.3 %all_to_all.32 = f32[12,48,128]{2,1,0:T(8,128)S(1)} all-to-all(f32[12,48,128]{2,1,0:T(8,128)S(1)} %broadcast_in_dim.6), channel_id=1, replica_groups=mesh['w'=4,'v'=3,'x'=4,'c'=2,'y'=8] {'x','v'}, dimensions={0} | all-to-all | bytes 589824 | tf_op jit(solution)/shard_map/all_to_all | solution.py:263
  71.9 6.4 %all_gather.6.halves_ref = f32[2,576,128]{2,1,0:T(8,128)S(1)} all-gather(f32[1,576,128]{2,1,0:T(8,128)S(1)} %bitcast.6), channel_id=1, replica_groups=mesh['w'=4,'v'=3,'x'=4,'c'=2,'y'=8] {'c'}, dimensions={0}, use_global_device_ids=true | all-gather | bytes 884736 | tf_op jit(solution)/shard_map/all_gather | solution.py:281
  78.3 0.8 shard_map.42
  79.1 17.7 %all_to_all.33 = f32[8,64,128]{2,1,0:T(8,128)S(1)} all-to-all(f32[8,64,128]{2,1,0:T(8,128)S(1)} %broadcast_in_dim.7), channel_id=1, replica_groups=mesh['w'=4,'v'=3,'x'=4,'c'=2,'y'=8] {'y'}, dimensions={0} | all-to-all | bytes 524288 | tf_op jit(solution)/shard_map/all_to_all | solution.py:263
  96.9 11.1 %all_to_all.34 = f32[12,64,128]{2,1,0:T(8,128)S(1)} all-to-all(f32[12,64,128]{2,1,0:T(8,128)S(1)} %broadcast_in_dim.8), channel_id=1, replica_groups=mesh['w'=4,'v'=3,'x'=4,'c'=2,'y'=8] {'x','v'}, dimensions={0} | all-to-all | bytes 786432 | tf_op jit(solution)/shard_map/all_to_all | solution.py:263
  108.0 0.0 copy-start.1
  108.0 5.4 %all_gather.7.strips_ref = f32[24,64,128]{2,1,0:T(8,128)S(1)} all-gather(f32[12,64,128]{2,1,0:T(8,128)S(1)} %all_to_all.34), channel_id=1, replica_groups=mesh['w'=4,'v'=3,'x'=4,'c'=2,'y'=8] {'c'}, dimensions={0}, use_global_device_ids=true | all-gather | bytes 1179648 | tf_op jit(solution)/shard_map/all_gather | solution.py:283
  113.4 5.3 %shard_map.43 = f32[4,16,256]{2,1,0:T(8,128)S(1)} custom-call(s32[4]{0:T(128)S(1)} %pad_add_fusion.place_ref, f32[24,64,128]{2,1,0:T(8,128)S(1)} %all_gather.7.strips_ref, f32[2,576,128]{2,1,0:T(8,128)S(1)} %all_gather.6.halves_ref), custom_call_target="tpu_custom_call" | custom-call | tf_op jit(solution)/shard_map/pallas_call | solution.py:227
  118.7 13.6 %all_to_all.35.got_ref = f32[4,16,256]{2,1,0:T(8,128)S(1)} all-to-all(f32[4,16,256]{2,1,0:T(8,128)S(1)} %shard_map.43), channel_id=1, replica_groups=mesh['w'=4,'v'=3,'x'=4,'c'=2,'y'=8] {'w'}, dimensions={0} | all-to-all | bytes 131072 | tf_op jit(solution)/shard_map/all_to_all | solution.py:263
  132.3 0.0 copy-done.1
  132.3 0.6 shard_map.44
  (5 shorter events, 0.1 us)
Async XLA Ops:
  0.7 0.7 copy-start
  3.4 14.9 %collective-permute-start = (f32[12,4,48,128]{3,2,1,0:T(8,128)S(1)}, f32[12,4,48,128]{3,2,1,0:T(8,128)S(1)}, u32[]{:S(2)}, u32[]{:S(2)}) collective-permute-start(f32[12,4,48,128]{3,2,1,0:T(8,128)S(1)} %get-tuple-element.5), channel_id=1, source_target_pairs={{0,8},{8,0},{1,9},{9,1},{2,10},{10,2},{3,11},{11,3},{4,12},{12,4},... | collective-permute-start | bytes 3538952 | tf_op jit(solution)/shard_map/ppermute | solution.py:277
  108.0 24.3 %copy-start.1 = (f32[24,256]{1,0:T(8,128)S(1)}, f32[24,256]{1,0:T(8,128)}, u32[]{:S(2)}) copy-start(f32[24,256]{1,0:T(8,128)} %momentum_ref.3) | copy-start | bytes 73732
